TPU v7x, 256 devices: a whole 4x4x8 slice. The times are simulated.
256 devices in a mesh: space: 32 (over z, x), state: 8 (over y, core).
Axes of the slice: x: 4, y: 4, z: 8, core: 2. Of those that a mesh axis runs over, the one named last changes fastest.
Arguments:
- states: float32 [64, 524288], P('state', 'space')
- bounds: float32 [3], replicated, as said below
- element_matrix: float32 [250, 125], replicated
- elem_nodes: int32 [125, 8192], P(None, 'space'), may hold values from 0 to 20479, as said below
- face_nodes: int32 [131072], P('space'), may hold values from 0 to 16383, as said below
- kinetic: float32 [8192], P('space'), may hold values from 0.5 to 4
- potential: float32 [8192], P('space'), may hold values from -1 to 0.5
- elem_count: int32 [32], P('space'), may hold values from 64 to 256, as said below
Outputs:
- filtered: float32 [64, 524288], P('state', 'space')
- margin: float32 [64, 64], P('state')
Inputs may be any that keep to these rules, and one draw needn't show every extreme that they name: `elem_nodes`: within each partition's 256 columns, rows 0 to 99 of a column are local node indices below 16384, and rows 100 to 124 are 16384 plus a face position below 4096. The entries of one column are distinct. `face_nodes`: within each partition's 4096 entries, distinct local node indices. `elem_count`: some partition has all 256 slots live in every draw. `bounds`: a0 < lo < hi.
All inputs are finite; a program needn't handle non-finite values.
Results may differ from a plain program's by a relative error of at most 0.0018.
Values may be sent and summed in bfloat16 or wider, within the bound.
A program may use at most 128 MiB of HBM per device.

v0:
```python
import jax
import jax.numpy as jnp
from jax import lax
from jax.sharding import PartitionSpec as P

DEG = 4


def shifted(value, axis, steps):
    count = lax.axis_size(axis)
    initial, last = (max(0, -steps), min(count, count - steps))
    return lax.ppermute(value, axis, [(source, source + steps) for source in range(initial, last)])


def hamiltonian(current, elem_nodes, face_nodes, kin_live, pot_live, element_matrix):
    width = current.shape[0]
    owned_count = current.shape[1]
    face_count = face_nodes.shape[0]
    corner_count = element_matrix.shape[1]
    face_vals = current[:, face_nodes]
    ghosts = shifted(face_vals.astype(jnp.bfloat16), "space", -1).astype(face_vals.dtype)
    extended = jnp.concatenate([current, ghosts], axis=1)
    gathered = extended[:, elem_nodes]
    product = jnp.einsum("kb,sbe->ske", element_matrix, gathered, precision=lax.Precision.HIGHEST)
    contrib = kin_live * product[:, :corner_count] + pot_live * product[:, corner_count:]
    summed = (
        jnp.zeros((width, owned_count + face_count), jnp.float32).at[:, elem_nodes].add(contrib)
    )
    returned = shifted(summed[:, owned_count:].astype(jnp.bfloat16), "space", 1).astype(jnp.float32)
    return summed[:, :owned_count].at[:, face_nodes].add(returned)


def body(states, bounds, element_matrix, elem_nodes, face_nodes, kinetic, potential, elem_count):
    slot_ids = jnp.arange(kinetic.shape[0], dtype=jnp.int32)
    alive = (slot_ids < elem_count[0]).astype(jnp.float32)
    kin_live = 0.5 * kinetic * alive
    pot_live = potential * alive

    def apply_operator(block):
        return hamiltonian(block, elem_nodes, face_nodes, kin_live, pot_live, element_matrix)

    lowest, lower, upper = (bounds[0], bounds[1], bounds[2])
    half_width = (upper - lower) / 2.0
    center = (upper + lower) / 2.0
    sigma_now = half_width / (lowest - center)
    gamma_ratio = 2.0 / sigma_now
    previous = states
    current = (apply_operator(states) - center * states) * (sigma_now / half_width)
    for repeat in range(DEG - 1):
        sigma_next = 1.0 / (gamma_ratio - sigma_now)
        following = (apply_operator(current) - center * current) * (
            2.0 * sigma_next / half_width
        ) - sigma_now * sigma_next * previous
        previous = current
        current = following
        sigma_now = sigma_next
    rounded = current.astype(jnp.bfloat16)
    node_total = current.shape[1] * lax.axis_size("space")
    partial_rows = lax.dot_general(
        rounded,
        lax.all_gather(rounded, "state", axis=0, tiled=True),
        (((1,), (1,)), ((), ())),
        preferred_element_type=jnp.float32,
    )
    margin = lax.psum(partial_rows, "space") / node_total
    return (current, margin)


def solution(mesh):
    in_specs = (
        P("state", "space"),
        P(),
        P(),
        P(None, "space"),
        P("space"),
        P("space"),
        P("space"),
        P("space"),
    )
    out_specs = (P("state", "space"), P("state", None))
    return jax.shard_map(body, mesh=mesh, in_specs=in_specs, out_specs=out_specs, check_vma=False)
```

profile of v0, /device:TPU:8, one launch (start us, length us, event | category | flops | bytes accessed | tf_op | source)
XLA Modules:
  0.0 1493.6 jit_solution(14101269677599258316)
XLA Ops:
  8.0 4.0 copy.113
  12.0 13.8 gather_fusion
  29.7 2.5 collective-permute-done
  33.3 5.4 copy.115
  38.7 63.1 %gather_fusion.1 = f32[32000,8]{1,0:T(8,128)} fusion(f32[8,20480]{0,1:T(8,128)} %copy.115, s32[32768]{0:T(1024)S(1)} %pad_clamp_fusion), kind=kCustom, calls=%fused_computation.1 | custom fusion | bytes 2176000 | tf_op jit(solution)/shard_map/gather | solution.py:23
  101.8 9.6 copy.116
  111.4 1.8 convolution_bitcast_fusion.3
  114.2 8.7 copy.118
  122.9 176.8 %scatter_custom_fusion = f32[8,20480]{0,1:T(8,128)} fusion(s32[32000]{0:T(1024)S(1)} %reshape.126, f32[32000,8]{1,0:T(8,128)} %copy.118, f32[]{:T(128)} %constant.7.clone.1), kind=kCustom, calls=%fused_computation.22 | custom fusion | flops 256000 | bytes 655872 | tf_op jit(solution)/shard_map/scatter-add | solution.py:27
  299.7 1.7 slice.99
  301.7 3.7 collective-permute-start.1
  309.4 5.7 slice.98
  315.2 2.0 copy.120
  317.2 27.0 %scatter_fusion = f32[8,16384]{0,1:T(8,128)} fusion(f32[8,16384]{0,1:T(8,128)} %slice.98, s32[4096]{0:T(1024)S(1)} %get-tuple-element.12, f32[4096,8]{1,0:T(8,128)} %copy.120), kind=kCustom, calls=%fused_computation.9 | custom fusion | flops 32768 | bytes 409600 | tf_op jit(solution)/shard_map/scatter-add | solution.py:30
  344.2 5.5 copy.121
  349.8 3.6 copy.122
  353.4 13.8 gather_fusion.2
  368.8 4.9 collective-permute-done.2
  373.7 5.4 copy.124
  379.1 63.1 %gather_fusion.3 = f32[32000,8]{1,0:T(8,128)} fusion(f32[8,20480]{0,1:T(8,128)} %copy.124, s32[32768]{0:T(1024)S(1)} %pad_clamp_fusion), kind=kCustom, calls=%fused_computation.3 | custom fusion | bytes 2176000 | tf_op jit(solution)/shard_map/gather | solution.py:23
  442.2 9.6 copy.125
  451.8 1.8 convolution_bitcast_fusion.2
  455.4 9.0 copy.127
  464.5 176.8 %scatter_custom_fusion.2 = f32[8,20480]{0,1:T(8,128)} fusion(s32[32000]{0:T(1024)S(1)} %reshape.126, f32[32000,8]{1,0:T(8,128)} %copy.127, f32[]{:T(128)} %constant.7.clone.1), kind=kCustom, calls=%fused_computation.20 | custom fusion | flops 256000 | bytes 655872 | tf_op jit(solution)/shard_map/scatter-add | solution.py:27
  641.3 1.7 slice.103
  643.3 4.7 collective-permute-start.3
  648.1 5.7 slice.102
  653.9 2.0 copy.129
  655.9 37.7 %scatter_fusion.1 = f32[8,16384]{0,1:T(8,128)} fusion(f32[8,16384]{0,1:T(8,128)} %slice.102, s32[4096]{0:T(1024)S(1)} %get-tuple-element.12, f32[4096,8]{1,0:T(8,128)} %copy.129), kind=kCustom, calls=%fused_computation.11 | custom fusion | flops 32768 | bytes 409600 | tf_op jit(solution)/shard_map/scatter-add | solution.py:30
  693.6 5.6 copy.130
  699.3 3.6 copy.131
  702.9 13.8 gather_fusion.4
  718.2 4.9 collective-permute-done.4
  723.2 5.4 copy.133
  728.6 63.1 %gather_fusion.5 = f32[32000,8]{1,0:T(8,128)} fusion(f32[8,20480]{0,1:T(8,128)} %copy.133, s32[32768]{0:T(1024)S(1)} %pad_clamp_fusion), kind=kCustom, calls=%fused_computation.5 | custom fusion | bytes 2176000 | tf_op jit(solution)/shard_map/gather | solution.py:23
  791.7 9.6 copy.134
  801.3 1.8 convolution_bitcast_fusion.1
  804.0 8.7 copy.136
  812.8 176.8 %scatter_custom_fusion.4 = f32[8,20480]{0,1:T(8,128)} fusion(s32[32000]{0:T(1024)S(1)} %reshape.126, f32[32000,8]{1,0:T(8,128)} %copy.136, f32[]{:T(128)} %constant.7.clone.1), kind=kCustom, calls=%fused_computation.18 | custom fusion | flops 256000 | bytes 655872 | tf_op jit(solution)/shard_map/scatter-add | solution.py:27
  989.6 1.7 slice.107
  991.6 4.1 collective-permute-start.5
  995.8 5.7 slice.106
  1001.5 2.0 copy.138
  1003.5 27.0 %scatter_fusion.2 = f32[8,16384]{0,1:T(8,128)} fusion(f32[8,16384]{0,1:T(8,128)} %slice.106, s32[4096]{0:T(1024)S(1)} %get-tuple-element.12, f32[4096,8]{1,0:T(8,128)} %copy.138), kind=kCustom, calls=%fused_computation.13 | custom fusion | flops 32768 | bytes 409600 | tf_op jit(solution)/shard_map/scatter-add | solution.py:30
  1030.5 5.5 copy.139
  1036.2 3.6 copy.140
  1039.8 13.8 gather_fusion.6
  1053.8 1.5 collective-permute-start.6
  1055.3 4.6 collective-permute-done.6
  1060.1 5.4 copy.142
  1065.4 63.1 %gather_fusion.7 = f32[32000,8]{1,0:T(8,128)} fusion(f32[8,20480]{0,1:T(8,128)} %copy.142, s32[32768]{0:T(1024)S(1)} %pad_clamp_fusion), kind=kCustom, calls=%fused_computation.7 | custom fusion | bytes 2176000 | tf_op jit(solution)/shard_map/gather | solution.py:23
  1128.5 9.6 copy.143
  1138.2 1.8 convolution_bitcast_fusion
  1141.8 9.0 copy.145
  1150.8 176.8 %scatter_custom_fusion.6 = f32[8,20480]{0,1:T(8,128)} fusion(s32[32000]{0:T(1024)S(1)} %reshape.126, f32[32000,8]{1,0:T(8,128)} %copy.145, f32[]{:T(128)} %constant.7.clone.1), kind=kCustom, calls=%fused_computation.16 | custom fusion | flops 256000 | bytes 655872 | tf_op jit(solution)/shard_map/scatter-add | solution.py:27
  1327.6 1.7 slice.111
  1329.6 4.0 collective-permute-start.7
  1333.8 5.7 slice.110
  1339.5 2.0 copy.147
  1341.5 27.0 %scatter_fusion.3 = f32[8,16384]{0,1:T(8,128)} fusion(f32[8,16384]{0,1:T(8,128)} %slice.110, s32[4096]{0:T(1024)S(1)} %get-tuple-element.12, f32[4096,8]{1,0:T(8,128)} %copy.147), kind=kCustom, calls=%fused_computation.15 | custom fusion | flops 32768 | bytes 409600 | tf_op jit(solution)/shard_map/scatter-add | solution.py:30
  1368.5 5.5 copy.148
  1375.1 33.3 %all-gather.2.cloned.1.call-done = bf16[64,16384]{1,0:T(8,128)(2,1)} async-done(((bf16[8,16384]{1,0:T(8,128)(2,1)}), bf16[64,16384]{1,0:T(8,128)(2,1)}) %all-gather.2.cloned.1.call-update) | async-done | bytes 2097168 | tf_op jit(solution)/shard_map/all_gather | solution.py:61
  1408.3 2.3 fusion.27
  1410.7 75.1 %psum.7 = f32[8,64]{1,0:T(8,128)S(1)} all-reduce(f32[8,64]{1,0:T(8,128)S(1)} %fusion.27), channel_id=1, replica_groups=mesh['space'=32,'state'=8] {'space'}, use_global_device_ids=true, to_apply=%region_8.0 | all-reduce | flops 512 | bytes 4096 | tf_op jit(solution)/shard_map/psum | solution.py:65
  (54 shorter events, 18.1 us)
Async XLA Ops:
  7.2 104.3 %copy-start = (f32[250,125]{1,0:T(8,128)S(1)}, f32[250,125]{1,0:T(8,128)}, u32[]{:S(2)}) copy-start(f32[250,125]{1,0:T(8,128)} %param.10) | copy-start | bytes 375004
  7.2 1401.2 %all-gather.2.cloned.1.call-start = ((), (), s32[]{:S(2)}) async-start(), calls=%async_computation | async-start | bytes 2359296 | tf_op jit(solution)/shard_map/all_gather | solution.py:61
  26.1 6.2 collective-permute-start
  122.9 182.5 %copy-start.2 = (f32[3]{0:T(128)S(1)}, f32[3]{0:T(128)}, u32[]{:S(2)}) copy-start(f32[3]{0:T(128)} %param.9) | copy-start | bytes 40
  301.7 13.4 collective-permute-start.1
  315.1 34.6 %copy-start.1 = (f32[8,16384]{1,0:T(8,128)S(1)}, f32[8,16384]{1,0:T(8,128)}, u32[]{:S(2)}) copy-start(f32[8,16384]{1,0:T(8,128)} %param.8) | copy-start | bytes 1572868
  367.5 6.2 collective-permute-start.2
  643.3 10.6 collective-permute-start.3
  716.9 6.2 collective-permute-start.4
  991.6 9.9 collective-permute-start.5
  1053.8 6.2 collective-permute-start.6
  1329.6 9.8 collective-permute-start.7
Sparse Core Ops, SparseCore 0:
  1375.2 33.0 all-gather.1
where the time goes:
time: 1500 us; the launch traced here: 1490 us
  other arithmetic  833 us (56%)
  local copies, waits for them, and re-layouts  484 us (32%)
  blocking collectives  75.1 us (5%)
  waiting for transfers between devices  50.2 us (3%)
  starting transfers between devices  21.9 us (1%)
  between operations  19.2 us (1%)
    scatter-add x4, other arithmetic, hamiltonian(): jnp.zeros((width, owned_count + face_count), jnp.float32).at[:, elem_nodes]  707 us
    gather x8, local copies, waits for them, and re-layouts, hamiltonian(): gathered = extended[:, elem_nodes]  291 us
    scatter-add x4, other arithmetic, hamiltonian(): return summed[:, :owned_count].at[:, face_nodes].add(returned)  119 us
    psum x1, blocking collectives, body(): margin = lax.psum(partial_rows, 'space') / node_total  75.1 us
    gather x4, local copies, waits for them, and re-layouts, hamiltonian(): face_vals = current[:, face_nodes]  55 us
    add x8, local copies, waits for them, and re-layouts, hamiltonian(): kin_live * product[:, :corner_count] + pot_live * product[:, corner_count:]  39.3 us
    all_gather x1, waiting for transfers between devices, body(): lax.all_gather(rounded, 'state', axis=0, tiled=True)  33.3 us
  transfers between devices with their start and end apart: 9, of which 5 were waited for; matrix products, arithmetic and copies ran while one was open for 2% of the time, Pallas kernels for 0%

commit v1 on v0

--- a/solution.py
+++ b/solution.py
@@ -4,6 +4,12 @@
 from jax.sharding import PartitionSpec as P
 
 DEG = 4
+
+
+def gather_and_add(x, name):
+    shards = lax.all_gather(x, name, axis=0, tiled=False)
+    result = shards.sum(axis=0)
+    return result
 
 
 def shifted(value, axis, steps):
@@ -62,7 +68,7 @@
         (((1,), (1,)), ((), ())),
         preferred_element_type=jnp.float32,
     )
-    margin = lax.psum(partial_rows, "space") / node_total
+    margin = gather_and_add(partial_rows, "space") / node_total
     return (current, margin)
 
 

time: 1500 us -> 1470 us (0.980)
  blocking collectives: 75.1 us -> 44.1 us
    psum x1 -> x0, blocking collectives: 75.1 us -> none  [body(): margin = lax.psum(partial_rows, 'space') / node_total]
    all_gather x0 -> x1, blocking collectives: none -> 44.1 us  [gather_and_add(): shards = lax.all_gather(x, name, axis=0, tiled=False)]
where the time goes in v1:
time: 1470 us; the launch traced here: 1460 us
  other arithmetic  833 us (57%)
  local copies, waits for them, and re-layouts  484 us (33%)
  waiting for transfers between devices  50.2 us (3%)
  blocking collectives  44.1 us (3%)
  starting transfers between devices  21.9 us (1%)
  between operations  19.2 us (1%)
    scatter-add x4, other arithmetic, hamiltonian(): jnp.zeros((width, owned_count + face_count), jnp.float32).at[:, elem_nodes]  707 us
    gather x8, local copies, waits for them, and re-layouts, hamiltonian(): gathered = extended[:, elem_nodes]  291 us
    scatter-add x4, other arithmetic, hamiltonian(): return summed[:, :owned_count].at[:, face_nodes].add(returned)  119 us
    gather x4, local copies, waits for them, and re-layouts, hamiltonian(): face_vals = current[:, face_nodes]  55 us
    all_gather x1, blocking collectives, gather_and_add(): shards = lax.all_gather(x, name, axis=0, tiled=False)  44.1 us
    add x8, local copies, waits for them, and re-layouts, hamiltonian(): kin_live * product[:, :corner_count] + pot_live * product[:, corner_count:]  39.3 us
    all_gather x1, waiting for transfers between devices, body(): lax.all_gather(rounded, 'state', axis=0, tiled=True)  33.3 us
  transfers between devices with their start and end apart: 9, of which 5 were waited for; matrix products, arithmetic and copies ran while one was open for 2% of the time, Pallas kernels for 0%

profile of v1, /device:TPU:8, one launch (start us, length us, event | category | flops | bytes accessed | tf_op | source)
XLA Modules:
  0.0 1462.6 jit_solution(17761905250028139426)
XLA Ops:
  8.0 4.0 copy.113
  12.0 13.8 gather_fusion
  29.7 2.5 collective-permute-done
  33.3 5.4 copy.115
  38.7 63.1 %gather_fusion.1 = f32[32000,8]{1,0:T(8,128)} fusion(f32[8,20480]{0,1:T(8,128)} %copy.115, s32[32768]{0:T(1024)S(1)} %pad_clamp_fusion), kind=kCustom, calls=%fused_computation.1 | custom fusion | bytes 2176000 | tf_op jit(solution)/shard_map/gather | solution.py:29
  101.8 9.6 copy.116
  111.4 1.8 convolution_bitcast_fusion.3
  114.2 8.7 copy.118
  122.9 176.8 %scatter_custom_fusion = f32[8,20480]{0,1:T(8,128)} fusion(s32[32000]{0:T(1024)S(1)} %reshape.126, f32[32000,8]{1,0:T(8,128)} %copy.118, f32[]{:T(128)} %constant.9.clone.1), kind=kCustom, calls=%fused_computation.22 | custom fusion | flops 256000 | bytes 655872 | tf_op jit(solution)/shard_map/scatter-add | solution.py:33
  299.7 1.7 slice.99
  301.7 3.7 collective-permute-start.1
  309.4 5.7 slice.98
  315.2 2.0 copy.120
  317.2 27.0 %scatter_fusion = f32[8,16384]{0,1:T(8,128)} fusion(f32[8,16384]{0,1:T(8,128)} %slice.98, s32[4096]{0:T(1024)S(1)} %get-tuple-element.12, f32[4096,8]{1,0:T(8,128)} %copy.120), kind=kCustom, calls=%fused_computation.9 | custom fusion | flops 32768 | bytes 409600 | tf_op jit(solution)/shard_map/scatter-add | solution.py:36
  344.2 5.5 copy.121
  349.8 3.6 copy.122
  353.4 13.8 gather_fusion.2
  368.8 4.9 collective-permute-done.2
  373.7 5.4 copy.124
  379.1 63.1 %gather_fusion.3 = f32[32000,8]{1,0:T(8,128)} fusion(f32[8,20480]{0,1:T(8,128)} %copy.124, s32[32768]{0:T(1024)S(1)} %pad_clamp_fusion), kind=kCustom, calls=%fused_computation.3 | custom fusion | bytes 2176000 | tf_op jit(solution)/shard_map/gather | solution.py:29
  442.2 9.6 copy.125
  451.8 1.8 convolution_bitcast_fusion.2
  455.4 9.0 copy.127
  464.5 176.8 %scatter_custom_fusion.2 = f32[8,20480]{0,1:T(8,128)} fusion(s32[32000]{0:T(1024)S(1)} %reshape.126, f32[32000,8]{1,0:T(8,128)} %copy.127, f32[]{:T(128)} %constant.9.clone.1), kind=kCustom, calls=%fused_computation.20 | custom fusion | flops 256000 | bytes 655872 | tf_op jit(solution)/shard_map/scatter-add | solution.py:33
  641.3 1.7 slice.103
  643.3 4.7 collective-permute-start.3
  648.1 5.7 slice.102
  653.9 2.0 copy.129
  655.9 37.7 %scatter_fusion.1 = f32[8,16384]{0,1:T(8,128)} fusion(f32[8,16384]{0,1:T(8,128)} %slice.102, s32[4096]{0:T(1024)S(1)} %get-tuple-element.12, f32[4096,8]{1,0:T(8,128)} %copy.129), kind=kCustom, calls=%fused_computation.11 | custom fusion | flops 32768 | bytes 409600 | tf_op jit(solution)/shard_map/scatter-add | solution.py:36
  693.6 5.6 copy.130
  699.3 3.6 copy.131
  702.9 13.8 gather_fusion.4
  718.2 4.9 collective-permute-done.4
  723.2 5.4 copy.133
  728.6 63.1 %gather_fusion.5 = f32[32000,8]{1,0:T(8,128)} fusion(f32[8,20480]{0,1:T(8,128)} %copy.133, s32[32768]{0:T(1024)S(1)} %pad_clamp_fusion), kind=kCustom, calls=%fused_computation.5 | custom fusion | bytes 2176000 | tf_op jit(solution)/shard_map/gather | solution.py:29
  791.7 9.6 copy.134
  801.3 1.8 convolution_bitcast_fusion.1
  804.0 8.7 copy.136
  812.8 176.8 %scatter_custom_fusion.4 = f32[8,20480]{0,1:T(8,128)} fusion(s32[32000]{0:T(1024)S(1)} %reshape.126, f32[32000,8]{1,0:T(8,128)} %copy.136, f32[]{:T(128)} %constant.9.clone.1), kind=kCustom, calls=%fused_computation.18 | custom fusion | flops 256000 | bytes 655872 | tf_op jit(solution)/shard_map/scatter-add | solution.py:33
  989.6 1.7 slice.107
  991.6 4.1 collective-permute-start.5
  995.8 5.7 slice.106
  1001.5 2.0 copy.138
  1003.5 27.0 %scatter_fusion.2 = f32[8,16384]{0,1:T(8,128)} fusion(f32[8,16384]{0,1:T(8,128)} %slice.106, s32[4096]{0:T(1024)S(1)} %get-tuple-element.12, f32[4096,8]{1,0:T(8,128)} %copy.138), kind=kCustom, calls=%fused_computation.13 | custom fusion | flops 32768 | bytes 409600 | tf_op jit(solution)/shard_map/scatter-add | solution.py:36
  1030.5 5.5 copy.139
  1036.2 3.6 copy.140
  1039.8 13.8 gather_fusion.6
  1053.8 1.5 collective-permute-start.6
  1055.3 4.6 collective-permute-done.6
  1060.1 5.4 copy.142
  1065.4 63.1 %gather_fusion.7 = f32[32000,8]{1,0:T(8,128)} fusion(f32[8,20480]{0,1:T(8,128)} %copy.142, s32[32768]{0:T(1024)S(1)} %pad_clamp_fusion), kind=kCustom, calls=%fused_computation.7 | custom fusion | bytes 2176000 | tf_op jit(solution)/shard_map/gather | solution.py:29
  1128.5 9.6 copy.143
  1138.2 1.8 convolution_bitcast_fusion
  1141.8 9.0 copy.145
  1150.8 176.8 %scatter_custom_fusion.6 = f32[8,20480]{0,1:T(8,128)} fusion(s32[32000]{0:T(1024)S(1)} %reshape.126, f32[32000,8]{1,0:T(8,128)} %copy.145, f32[]{:T(128)} %constant.9.clone.1), kind=kCustom, calls=%fused_computation.16 | custom fusion | flops 256000 | bytes 655872 | tf_op jit(solution)/shard_map/scatter-add | solution.py:33
  1327.6 1.7 slice.111
  1329.6 4.0 collective-permute-start.7
  1333.8 5.7 slice.110
  1339.5 2.0 copy.147
  1341.5 27.0 %scatter_fusion.3 = f32[8,16384]{0,1:T(8,128)} fusion(f32[8,16384]{0,1:T(8,128)} %slice.110, s32[4096]{0:T(1024)S(1)} %get-tuple-element.12, f32[4096,8]{1,0:T(8,128)} %copy.147), kind=kCustom, calls=%fused_computation.15 | custom fusion | flops 32768 | bytes 409600 | tf_op jit(solution)/shard_map/scatter-add | solution.py:36
  1368.5 5.5 copy.148
  1375.1 33.3 %all-gather.3.cloned.1.call-done = bf16[64,16384]{1,0:T(8,128)(2,1)} async-done(((bf16[8,16384]{1,0:T(8,128)(2,1)}), bf16[64,16384]{1,0:T(8,128)(2,1)}) %all-gather.3.cloned.1.call-update) | async-done | bytes 2097168 | tf_op jit(solution)/shard_map/all_gather | solution.py:67
  1408.3 2.3 fusion.27
  1410.7 44.1 %all-gather = f32[256,64]{1,0:T(8,128)S(1)} all-gather(f32[8,64]{1,0:T(8,128)S(1)} %fusion.27), channel_id=2, replica_groups=mesh['space'=32,'state'=8] {'space'}, dimensions={0}, use_global_device_ids=true | all-gather | bytes 67584 | tf_op jit(solution)/shard_map/all_gather | solution.py:10
  (55 shorter events, 18.1 us)
Async XLA Ops:
  7.2 104.3 %copy-start = (f32[250,125]{1,0:T(8,128)S(1)}, f32[250,125]{1,0:T(8,128)}, u32[]{:S(2)}) copy-start(f32[250,125]{1,0:T(8,128)} %param.10) | copy-start | bytes 375004
  7.2 1401.2 %all-gather.3.cloned.1.call-start = ((), (), s32[]{:S(2)}) async-start(), calls=%async_computation | async-start | bytes 2359296 | tf_op jit(solution)/shard_map/all_gather | solution.py:67
  26.1 6.2 collective-permute-start
  122.9 182.5 %copy-start.2 = (f32[3]{0:T(128)S(1)}, f32[3]{0:T(128)}, u32[]{:S(2)}) copy-start(f32[3]{0:T(128)} %param.9) | copy-start | bytes 40
  301.7 13.4 collective-permute-start.1
  315.1 34.6 %copy-start.1 = (f32[8,16384]{1,0:T(8,128)S(1)}, f32[8,16384]{1,0:T(8,128)}, u32[]{:S(2)}) copy-start(f32[8,16384]{1,0:T(8,128)} %param.8) | copy-start | bytes 1572868
  367.5 6.2 collective-permute-start.2
  643.3 10.6 collective-permute-start.3
  716.9 6.2 collective-permute-start.4
  991.6 9.9 collective-permute-start.5
  1053.8 6.2 collective-permute-start.6
  1329.6 9.8 collective-permute-start.7
Sparse Core Ops, SparseCore 0:
  1375.2 33.0 all-gather.2
